TPU v7x, 256 devices: a whole 4x4x8 slice. The times are simulated.
256 devices in a mesh: shot: 8 (over y, core), band: 32 (over x, z).
Axes of the slice: x: 4, y: 4, z: 8, core: 2. Of those that a mesh axis runs over, the one named last changes fastest.
Arguments:
- sensitivity: bfloat16 [16384, 128, 128], P(('shot', 'band')), may hold values from -0.0625 to 0.0625
- bundle_of: int32 [16384], P(('shot', 'band')), may hold values from 0 to 31
- cellblock_of: int32 [16384], P(('shot', 'band')), may hold values from 0 to 15
- state: float32 [65536, 128], P('band'), may hold values from -6 to 6
- prior_velocity: float32 [65536, 128], P('band'), may hold values from -6 to 6
- observed: float32 [256, 128], P(('shot', 'band')), may hold values from -6 to 6
- pick_weight: float32 [256, 128], P(('shot', 'band')), may hold values from 0.3 to 3
Outputs:
- new_state: float32 [65536, 128], P('band')
- weighted_residual: float32 [256, 128, 128], P(('shot', 'band'))
Inputs may be any that keep to these rules, and one draw needn't show every extreme that they name: bundle_of names a bundle of the block's own source group. cellblock_of names a cell block of the block's own depth band.
All inputs are finite; a program needn't handle non-finite values.
Results may differ from a plain program's by a relative error of at most 0.0059.
Values may be sent and summed in bfloat16 or wider, within the bound.
A program may use at most 64 MiB of HBM per device.

v0:
```python
import jax
import jax.numpy as jnp
from jax import lax
from jax.sharding import PartitionSpec as P

CBLK = 128


def block_products(sensitivity, cellblock_of, probe):
    columns = probe.reshape(-1, CBLK, probe.shape[1])[cellblock_of]
    return jnp.einsum("krc,kce->kre", sensitivity, columns, preferred_element_type=jnp.float32)


def adjoint_part(sensitivity, bundle_of, cellblock_of, resid_all, cell_blocks):
    rows = resid_all[bundle_of]
    contrib = jnp.einsum("krc,kre->kce", sensitivity, rows, preferred_element_type=jnp.float32)
    summed = jax.ops.segment_sum(contrib, cellblock_of, num_segments=cell_blocks)
    return summed.reshape(cell_blocks * CBLK, rows.shape[2])


def per_device(sensitivity, bundle_of, cellblock_of, state, prior_velocity, observed, pick_weight):
    nband = lax.axis_size("band")
    owned = observed.shape[0]
    bundles = owned * nband
    cell_blocks = state.shape[0] // CBLK

    def residual_pass(probe):
        prod = block_products(sensitivity, cellblock_of, probe)
        partial_value = jax.ops.segment_sum(prod, bundle_of, num_segments=bundles)
        pred = lax.psum_scatter(partial_value, "band", scatter_dimension=0, tiled=True)
        resid = pick_weight[:, :, None] * (pred - observed[:, :, None])
        resid_all = lax.all_gather(resid.astype(jnp.bfloat16), "band", axis=0, tiled=True)
        return (resid, adjoint_part(sensitivity, bundle_of, cellblock_of, resid_all, cell_blocks))

    probe1 = (state + 0.5 * prior_velocity).astype(jnp.bfloat16)
    res1, part1 = residual_pass(probe1)

    def summed_grad(part):
        return lax.psum(part, "shot")

    grad1 = summed_grad(part1)
    middle = state + 0.5 * (prior_velocity - 0.5 * grad1)
    probe2 = (middle + 0.5 * prior_velocity).astype(jnp.bfloat16)
    res2, part2 = residual_pass(probe2)
    grad2 = summed_grad(part2)
    new_state = state + 0.5 * (prior_velocity - 0.25 * (grad1 + grad2))
    return (new_state, res2)


def solution(mesh):
    in_specs = (
        P(("shot", "band"), None, None),
        P(("shot", "band")),
        P(("shot", "band")),
        P("band", None),
        P("band", None),
        P(("shot", "band"), None),
        P(("shot", "band"), None),
    )
    out_specs = (P("band", None), P(("shot", "band"), None, None))
    return jax.shard_map(
        per_device, mesh=mesh, in_specs=in_specs, out_specs=out_specs, check_vma=False
    )
```

profile of v0, /device:TPU:2, one launch (start us, length us, event | category | flops | bytes accessed | tf_op | source)
XLA Modules:
  0.0 845.8 jit_solution(9297075635177994917)
XLA Ops:
  7.2 0.8 compare_select_fusion.1
  8.0 1.7 add_convert_fusion.1
  9.7 2.2 gather_fusion
  11.8 5.2 convolution_bitcast_fusion.3
  17.0 5.6 copy.28
  22.6 1.6 broadcast.21.clone
  24.2 13.5 %scatter_fusion = f32[32,128,128]{2,1,0:T(8,128)} fusion(f32[32,128,128]{2,1,0:T(8,128)} %broadcast.21.clone, s32[64]{0:T(128)S(1)} %copy-done.3, f32[64,128,128]{2,1,0:T(8,128)} %copy.28), kind=kCustom, calls=%fused_computation.4 | custom fusion | flops 1048576 | bytes 12583168 | tf_op jit(solution)/shard_map/scatter-add | solution.py:29
  37.8 218.6 %reduce-scatter.3.cloned.1.call-done = f32[1,128,128]{2,1,0:T(8,128)} async-done(((f32[32,128,128]{2,1,0:T(8,128)}), f32[1,128,128]{2,1,0:T(8,128)}) %reduce-scatter.3.cloned.1.call-update) | async-done | bytes 65552 | tf_op jit(solution)/shard_map/reduce_scatter | solution.py:30
  256.4 1.6 multiply_convert_fusion
  258.0 76.1 %all-gather.3.cloned.1.call-done = bf16[32,128,128]{2,1,0:T(8,128)(2,1)} async-done(((bf16[1,128,128]{2,1,0:T(8,128)(2,1)}), bf16[32,128,128]{2,1,0:T(8,128)(2,1)}) %all-gather.3.cloned.1.call-update) | async-done | bytes 1048592 | tf_op jit(solution)/shard_map/all_gather | solution.py:32
  334.1 3.4 gather_fusion.1
  337.5 4.4 convolution_bitcast_fusion.2
  341.9 5.6 copy.30
  347.6 8.8 %scatter_fusion.1 = f32[16,128,128]{2,1,0:T(8,128)S(1)} fusion(f32[16,128,128]{2,1,0:T(8,128)S(1)} %broadcast.20.clone, s32[64]{0:T(128)S(1)} %copy-done.6, f32[64,128,128]{2,1,0:T(8,128)} %copy.30), kind=kCustom, calls=%fused_computation.5 | custom fusion | flops 1048576 | bytes 12583168 | tf_op jit(solution)/shard_map/scatter-add | solution.py:17
  356.4 1.0 copy-done.2
  357.5 66.3 %all-reduce.3.cloned.1.call-done = f32[2048,128]{1,0:T(8,128)} async-done(((f32[2048,128]{1,0:T(8,128)}), f32[2048,128]{1,0:T(8,128)}) %all-reduce.3.cloned.1.call-update) | async-done | bytes 1048592 | tf_op jit(solution)/shard_map/psum | solution.py:39
  423.8 2.1 add_convert_fusion
  425.9 2.2 gather_fusion.2
  428.0 5.2 convolution_bitcast_fusion.1
  433.2 5.6 copy.32
  438.8 1.6 broadcast.21
  440.4 13.5 %scatter_fusion.2 = f32[32,128,128]{2,1,0:T(8,128)} fusion(f32[32,128,128]{2,1,0:T(8,128)} %broadcast.21, s32[64]{0:T(128)S(1)} %copy-done.3, f32[64,128,128]{2,1,0:T(8,128)} %copy.32), kind=kCustom, calls=%fused_computation.6 | custom fusion | flops 1048576 | bytes 12583168 | tf_op jit(solution)/shard_map/scatter-add | solution.py:29
  454.0 214.7 %reduce-scatter.5.cloned.1.call-done = f32[1,128,128]{2,1,0:T(8,128)} async-done(((f32[32,128,128]{2,1,0:T(8,128)}), f32[1,128,128]{2,1,0:T(8,128)}) %reduce-scatter.5.cloned.1.call-update) | async-done | bytes 65552 | tf_op jit(solution)/shard_map/reduce_scatter | solution.py:30
  668.7 1.6 fusion
  670.5 75.5 %all-gather.5.cloned.1.call-done = bf16[32,128,128]{2,1,0:T(8,128)(2,1)} async-done(((bf16[1,128,128]{2,1,0:T(8,128)(2,1)}), bf16[32,128,128]{2,1,0:T(8,128)(2,1)}) %all-gather.5.cloned.1.call-update) | async-done | bytes 1048592 | tf_op jit(solution)/shard_map/all_gather | solution.py:32
  746.0 3.4 gather_fusion.3
  749.4 4.4 convolution_bitcast_fusion
  753.8 5.6 copy.34
  759.5 8.8 %scatter_fusion.3 = f32[16,128,128]{2,1,0:T(8,128)S(1)} fusion(f32[16,128,128]{2,1,0:T(8,128)S(1)} %broadcast.20, s32[64]{0:T(128)S(1)} %copy-done.6, f32[64,128,128]{2,1,0:T(8,128)} %copy.34), kind=kCustom, calls=%fused_computation.7 | custom fusion | flops 1048576 | bytes 12583168 | tf_op jit(solution)/shard_map/scatter-add | solution.py:17
  768.3 1.0 copy-done.1
  769.3 66.3 %all-reduce.5.cloned.1.call-done = f32[2048,128]{1,0:T(8,128)} async-done(((f32[2048,128]{1,0:T(8,128)}), f32[2048,128]{1,0:T(8,128)}) %all-reduce.5.cloned.1.call-update) | async-done | bytes 1048592 | tf_op jit(solution)/shard_map/psum | solution.py:39
  835.6 3.3 multiply_add_fusion
  (29 shorter events, 0.8 us)
Async XLA Ops:
  7.2 4.7 copy-start
  7.2 249.2 %reduce-scatter.3.cloned.1.call-start = ((), (), s32[]{:S(2)}) async-start(), calls=%async_computation.2 | async-start | bytes 2162688 | tf_op jit(solution)/shard_map/reduce_scatter | solution.py:30
  22.6 1.6 copy-start.3
  37.7 218.6 %copy-start.4 = (f32[1,128]{1,0:T(1,128)S(1)}, f32[1,128]{1,0:T(1,128)}, u32[]{:S(2)}) copy-start(f32[1,128]{1,0:T(1,128)} %param.12) | copy-start | bytes 1540
  37.7 218.6 %copy-start.5 = (f32[1,128]{1,0:T(1,128)S(1)}, f32[1,128]{1,0:T(1,128)}, u32[]{:S(2)}) copy-start(f32[1,128]{1,0:T(1,128)} %param.13) | copy-start | bytes 1540
  37.7 296.4 %all-gather.3.cloned.1.call-start = ((), (), s32[]{:S(2)}) async-start(), calls=%async_computation.3 | async-start | bytes 1081344 | tf_op jit(solution)/shard_map/all_gather | solution.py:32
  257.9 165.8 %all-reduce.3.cloned.1.call-start = ((), (), s32[]{:S(2)}) async-start(), calls=%async_computation.4 | async-start | bytes 2097152 | tf_op jit(solution)/shard_map/psum | solution.py:39
  341.9 5.7 copy-start.6
  356.4 1.0 copy-start.2
  357.4 311.3 %reduce-scatter.5.cloned.1.call-start = ((), (), s32[]{:S(2)}) async-start(), calls=%async_computation.5 | async-start | bytes 2162688 | tf_op jit(solution)/shard_map/reduce_scatter | solution.py:30
  453.9 292.1 %all-gather.5.cloned.1.call-start = ((), (), s32[]{:S(2)}) async-start(), calls=%async_computation.6 | async-start | bytes 1081344 | tf_op jit(solution)/shard_map/all_gather | solution.py:32
  670.3 165.3 %all-reduce.5.cloned.1.call-start = ((), (), s32[]{:S(2)}) async-start(), calls=%async_computation.7 | async-start | bytes 2097152 | tf_op jit(solution)/shard_map/psum | solution.py:39
  768.3 1.0 copy-start.1
Sparse Core Ops, SparseCore 0:
  37.9 218.4 reduce-scatter.2
  259.9 74.2 all-gather.2
  357.5 66.1 all-reduce.2
  454.0 214.5 reduce-scatter.4
  671.7 74.3 all-gather.4
  769.4 66.1 all-reduce.4
where the time goes:
time: 847 us; the launch traced here: 846 us
  waiting for transfers between devices  718 us (85%)
  other arithmetic  55.7 us (7%)
  local copies, waits for them, and re-layouts  38.7 us (5%)
  matrix products  19.1 us (2%)
  between operations  14.2 us (2%)
    reduce_scatter x2, waiting for transfers between devices, residual_pass(): lax.psum_scatter(partial_value, 'band', scatter_dimension=0, tiled=True)  433 us
    all_gather x2, waiting for transfers between devices, residual_pass(): lax.all_gather(resid.astype(jnp.bfloat16), 'band', axis=0, tiled=True)  152 us
    psum x2, waiting for transfers between devices, summed_grad(): return lax.psum(part, 'shot')  133 us
    scatter-add x2, other arithmetic, residual_pass(): partial_value = jax.ops.segment_sum(prod, bundle_of, num_segments=bundles)  27 us
    scatter-add x2, other arithmetic, adjoint_part(): jax.ops.segment_sum(contrib, cellblock_of, num_segments=cell_blocks)  17.6 us
  transfers between devices with their start and end apart: 6, of which 6 were waited for; matrix products, arithmetic and copies ran while one was open for 0% of the time, Pallas kernels for 0%

commit v1 on v0

--- a/solution.py
+++ b/solution.py
@@ -29,7 +29,12 @@
         partial_value = jax.ops.segment_sum(prod, bundle_of, num_segments=bundles)
         pred = lax.psum_scatter(partial_value, "band", scatter_dimension=0, tiled=True)
         resid = pick_weight[:, :, None] * (pred - observed[:, :, None])
-        resid_all = lax.all_gather(resid.astype(jnp.bfloat16), "band", axis=0, tiled=True)
+        shard = resid.astype(jnp.bfloat16)
+        devices = lax.axis_size("band")
+        repeats = [devices if d == 0 else 1 for d in range(shard.ndim)]
+        resid_all = lax.all_to_all(
+            jnp.tile(shard, repeats), "band", split_axis=0, concat_axis=0, tiled=True
+        )
         return (resid, adjoint_part(sensitivity, bundle_of, cellblock_of, resid_all, cell_blocks))
 
     probe1 = (state + 0.5 * prior_velocity).astype(jnp.bfloat16)

time: 847 us -> 751 us (0.89)
  waiting for transfers between devices: 718 us -> 586 us
  blocking collectives: 0 us -> 28.7 us
    all_gather x2 -> x0, waiting for transfers between devices: 152 us -> none  [residual_pass(): lax.all_gather(resid.astype(jnp.bfloat16), 'band', axis=0, tiled=True)]
    all_to_all x0 -> x1, blocking collectives: none -> 28.7 us  [residual_pass(): lax.all_to_all(jnp.tile(shard, repeats), 'band', split_axis=0, concat_axi...]
    all_to_all x0 -> x1, waiting for transfers between devices: none -> 20.8 us  [residual_pass(): lax.all_to_all(jnp.tile(shard, repeats), 'band', split_axis=0, concat_axi...]
  transfers between devices with their start and end apart: 6 -> 5, of which waited for: 6 -> 5; matrix products, arithmetic and copies ran while one was open for 0% -> 0% of each run, Pallas kernels for 0% -> 0%
where the time goes in v1:
time: 751 us; the launch traced here: 749 us
  waiting for transfers between devices  586 us (78%)
  other arithmetic  55.1 us (7%)
  local copies, waits for them, and re-layouts  37.7 us (5%)
  blocking collectives  28.7 us (4%)
  matrix products  19.1 us (3%)
  between operations  13.9 us (2%)
  starting transfers between devices  8.2 us (1%)
    reduce_scatter x2, waiting for transfers between devices, residual_pass(): lax.psum_scatter(partial_value, 'band', scatter_dimension=0, tiled=True)  433 us
    psum x2, waiting for transfers between devices, summed_grad(): return lax.psum(part, 'shot')  133 us
    all_to_all x1, blocking collectives, residual_pass(): lax.all_to_all(jnp.tile(shard, repeats), 'band', split_axis=0, concat_axi...  28.7 us
    scatter-add x2, other arithmetic, residual_pass(): partial_value = jax.ops.segment_sum(prod, bundle_of, num_segments=bundles)  27.1 us
    all_to_all x1, waiting for transfers between devices, residual_pass(): lax.all_to_all(jnp.tile(shard, repeats), 'band', split_axis=0, concat_axi...  20.8 us
    scatter-add x2, other arithmetic, adjoint_part(): jax.ops.segment_sum(contrib, cellblock_of, num_segments=cell_blocks)  17.6 us
  transfers between devices with their start and end apart: 5, of which 5 were waited for; matrix products, arithmetic and copies ran while one was open for 0% of the time, Pallas kernels for 0%

profile of v1, /device:TPU:2, one launch (start us, length us, event | category | flops | bytes accessed | tf_op | source)
XLA Modules:
  0.0 749.1 jit_solution(2963647071339239053)
XLA Ops:
  8.0 1.7 add_convert_fusion.1
  9.7 2.2 gather_fusion
  11.9 5.2 convolution_bitcast_fusion.3
  17.0 5.6 copy.14
  22.6 1.6 broadcast.25.clone
  24.2 13.5 %scatter_fusion = f32[32,128,128]{2,1,0:T(8,128)} fusion(f32[32,128,128]{2,1,0:T(8,128)} %broadcast.25.clone, s32[64]{0:T(128)S(1)} %copy-done.3, f32[64,128,128]{2,1,0:T(8,128)} %copy.14), kind=kCustom, calls=%fused_computation.4 | custom fusion | flops 1048576 | bytes 12583168 | tf_op jit(solution)/shard_map/scatter-add | solution.py:29
  37.8 218.0 %reduce-scatter.3.cloned.1.call-done = f32[1,128,128]{2,1,0:T(8,128)} async-done(((f32[32,128,128]{2,1,0:T(8,128)}), f32[1,128,128]{2,1,0:T(8,128)}) %reduce-scatter.3.cloned.1.call-update) | async-done | bytes 65552 | tf_op jit(solution)/shard_map/reduce_scatter | solution.py:30
  256.7 1.2 tile.9
  257.9 8.0 %all-to-all-start = ((bf16[32,128,128]{2,1,0:T(8,128)(2,1)}), bf16[32,128,128]{2,1,0:T(8,128)(2,1)S(1)}, u32[]{:S(2)}, u32[]{:S(2)}) async-start(bf16[32,128,128]{2,1,0:T(8,128)(2,1)} %tile.9), calls=%async_computation.1 | async-start | bytes 2097152 | tf_op jit(solution)/shard_map/all_to_all | solution.py:35
  266.1 20.8 %all-to-all-done = bf16[32,128,128]{2,1,0:T(8,128)(2,1)S(1)} async-done(((bf16[32,128,128]{2,1,0:T(8,128)(2,1)}), bf16[32,128,128]{2,1,0:T(8,128)(2,1)S(1)}, u32[]{:S(2)}, u32[]{:S(2)}) %all-to-all-start) | async-done | bytes 1048608 | tf_op jit(solution)/shard_map/all_to_all | solution.py:35
  286.9 2.1 gather_fusion.1
  289.0 4.4 convolution_bitcast_fusion.2
  293.4 5.6 copy.16
  299.1 8.8 %scatter_fusion.1 = f32[16,128,128]{2,1,0:T(8,128)S(1)} fusion(f32[16,128,128]{2,1,0:T(8,128)S(1)} %broadcast.24.clone, s32[64]{0:T(128)S(1)} %copy-done.6, f32[64,128,128]{2,1,0:T(8,128)} %copy.16), kind=kCustom, calls=%fused_computation.5 | custom fusion | flops 1048576 | bytes 12583168 | tf_op jit(solution)/shard_map/scatter-add | solution.py:17
  308.0 1.0 copy-done.2
  309.0 66.4 %all-reduce.3.cloned.1.call-done = f32[2048,128]{1,0:T(8,128)} async-done(((f32[2048,128]{1,0:T(8,128)}), f32[2048,128]{1,0:T(8,128)}) %all-reduce.3.cloned.1.call-update) | async-done | bytes 1048592 | tf_op jit(solution)/shard_map/psum | solution.py:44
  375.4 2.1 add_convert_fusion
  377.5 2.2 gather_fusion.2
  379.7 5.2 convolution_bitcast_fusion.1
  384.9 5.6 copy.18
  390.5 1.6 broadcast.25
  392.1 13.5 %scatter_fusion.2 = f32[32,128,128]{2,1,0:T(8,128)} fusion(f32[32,128,128]{2,1,0:T(8,128)} %broadcast.25, s32[64]{0:T(128)S(1)} %copy-done.3, f32[64,128,128]{2,1,0:T(8,128)} %copy.18), kind=kCustom, calls=%fused_computation.6 | custom fusion | flops 1048576 | bytes 12583168 | tf_op jit(solution)/shard_map/scatter-add | solution.py:29
  405.7 214.6 %reduce-scatter.5.cloned.1.call-done = f32[1,128,128]{2,1,0:T(8,128)} async-done(((f32[32,128,128]{2,1,0:T(8,128)}), f32[1,128,128]{2,1,0:T(8,128)}) %reduce-scatter.5.cloned.1.call-update) | async-done | bytes 65552 | tf_op jit(solution)/shard_map/reduce_scatter | solution.py:30
  620.3 1.6 convert_bitcast_fusion
  622.1 28.7 %all_to_all.10 = bf16[32,128,128]{2,1,0:T(8,128)(2,1)S(1)} all-to-all(bf16[32,128,128]{2,1,0:T(8,128)(2,1)S(1)} %tile.21), channel_id=1, replica_groups=mesh['shot'=8,'band'=32] {'band'}, dimensions={0} | all-to-all | bytes 2097152 | tf_op jit(solution)/shard_map/all_to_all | solution.py:35
  650.8 2.1 gather_fusion.3
  652.9 4.4 convolution_bitcast_fusion
  657.3 5.6 copy.20
  663.0 8.8 %scatter_fusion.3 = f32[16,128,128]{2,1,0:T(8,128)S(1)} fusion(f32[16,128,128]{2,1,0:T(8,128)S(1)} %broadcast.24, s32[64]{0:T(128)S(1)} %copy-done.6, f32[64,128,128]{2,1,0:T(8,128)} %copy.20), kind=kCustom, calls=%fused_computation.7 | custom fusion | flops 1048576 | bytes 12583168 | tf_op jit(solution)/shard_map/scatter-add | solution.py:17
  671.8 1.0 copy-done.1
  672.8 66.5 %all-reduce.5.cloned.1.call-done = f32[2048,128]{1,0:T(8,128)} async-done(((f32[2048,128]{1,0:T(8,128)}), f32[2048,128]{1,0:T(8,128)}) %all-reduce.5.cloned.1.call-update) | async-done | bytes 1048592 | tf_op jit(solution)/shard_map/psum | solution.py:44
  739.3 3.3 multiply_add_fusion
  (28 shorter events, 2.4 us)
Async XLA Ops:
  7.2 4.7 copy-start
  7.2 248.6 %reduce-scatter.3.cloned.1.call-start = ((), (), s32[]{:S(2)}) async-start(), calls=%async_computation.4 | async-start | bytes 2162688 | tf_op jit(solution)/shard_map/reduce_scatter | solution.py:30
  22.6 1.6 copy-start.3
  37.7 218.0 %copy-start.4 = (f32[1,128]{1,0:T(1,128)S(1)}, f32[1,128]{1,0:T(1,128)}, u32[]{:S(2)}) copy-start(f32[1,128]{1,0:T(1,128)} %param.12) | copy-start | bytes 1540
  37.8 218.0 %copy-start.5 = (f32[1,128]{1,0:T(1,128)S(1)}, f32[1,128]{1,0:T(1,128)}, u32[]{:S(2)}) copy-start(f32[1,128]{1,0:T(1,128)} %param.13) | copy-start | bytes 1540
  257.9 29.0 %all-to-all-start = ((bf16[32,128,128]{2,1,0:T(8,128)(2,1)}), bf16[32,128,128]{2,1,0:T(8,128)(2,1)S(1)}, u32[]{:S(2)}, u32[]{:S(2)}) async-start(bf16[32,128,128]{2,1,0:T(8,128)(2,1)} %tile.9), calls=%async_computation.1 | async-start | bytes 2097152 | tf_op jit(solution)/shard_map/all_to_all | solution.py:35
  266.0 109.5 %all-reduce.3.cloned.1.call-start = ((), (), s32[]{:S(2)}) async-start(), calls=%async_computation.5 | async-start | bytes 2097152 | tf_op jit(solution)/shard_map/psum | solution.py:44
  293.4 5.7 copy-start.6
  307.9 1.0 copy-start.2
  308.9 311.3 %reduce-scatter.5.cloned.1.call-start = ((), (), s32[]{:S(2)}) async-start(), calls=%async_computation.6 | async-start | bytes 2162688 | tf_op jit(solution)/shard_map/reduce_scatter | solution.py:30
  405.6 333.6 %all-reduce.5.cloned.1.call-start = ((), (), s32[]{:S(2)}) async-start(), calls=%async_computation.7 | async-start | bytes 2097152 | tf_op jit(solution)/shard_map/psum | solution.py:44
  671.8 1.0 copy-start.1
Sparse Core Ops, SparseCore 0:
  37.9 217.8 reduce-scatter.2
  309.1 66.3 all-reduce.2
  405.7 214.4 reduce-scatter.4
  672.9 66.2 all-reduce.4
